TPU v7x, 32 devices: a whole 2x2x4 slice. The times are simulated.
32 devices in a mesh: lat: 8 (over y, x, core), lon: 4 (over z).
Axes of the slice: x: 2, y: 2, z: 4, core: 2. Of those that a mesh axis runs over, the one named last changes fastest.
Arguments:
- height: float32 [2048, 8640], P('lat', 'lon'), may hold values from -6 to 8
- east_vel: float32 [2048, 8640], P('lat', 'lon'), may hold values from -3 to 3
- north_vel: float32 [2048, 8640], P('lat', 'lon'), may hold values from -3 to 3
- sea_depth: float32 [2048, 8640], P('lat', 'lon'), may hold values from 1 to 4
- sea_mask: int32 [2048, 8640], P('lat', 'lon'), may hold values 0 or 1
- forcing: bfloat16 [2, 8, 2048, 8640], P(None, None, 'lat', 'lon'), may hold values from -6 to 6
- thickness: float32 [8], replicated, may hold values from 1 to 10
- cycle_length: int32 [2048], P('lat'), may hold values from 180 to 720
- slot_order: int32 [720], replicated, may hold values from 0 to 719, each once
- love_index: int32 [720], replicated, may hold values from 0 to 63
- love_table: float32 [64], replicated, may hold values from 0.5 to 1.5
Outputs:
- height_out: float32 [2048, 8640], P('lat', 'lon')
- east_out: float32 [2048, 8640], P('lat', 'lon')
- north_out: float32 [2048, 8640], P('lat', 'lon')
- load_coeffs: float32 [2, 720, 720], P(None, 'lon', 'lat')
- sal_field: float32 [2048, 8640], P('lat', 'lon')
Inputs may be any that keep to these rules, and one draw needn't show every extreme that they name: `slot_order`: every order appears once.
All inputs are finite; a program needn't handle non-finite values. No bound on the sum of `sea_mask` on one device may be relied on, other than what follows from the above.
Results may differ from a plain program's by a relative error of at most 0.014.
Values may be sent and summed in bfloat16 or wider, within the bound.
No kernel may reach another device: no remote copies, remote signals or barrier semaphores. Data moves between devices by JAX's collectives and lax.ppermute only.
A program may use at most 192 MiB of HBM per device.

v0:
```python
import math
import jax
import jax.numpy as jnp
from jax import lax
from jax.sharding import PartitionSpec as P

NLON = 8640
LMAX = 720
LEVELS = 8
ITERS = 10
LOVE_ROWS = 64
time_step = 0.6
drag_coeff = 0.5
tide_speed = 0.1
coriolis_scale = 0.8
degree_block = 24
rescale_limit = 1e20
rescale_log = 20.0 * math.log(10.0)


def padded(block, sides, width, periodic):
    for axis, dim in sides:
        count = lax.axis_size(axis)
        forward = [(i, i + 1) for i in range(count - 1)]
        if periodic:
            forward.append((count - 1, 0))
        backward = [(target, source) for source, target in forward]
        low = lax.ppermute(
            lax.slice_in_dim(block, block.shape[dim] - width, None, axis=dim), axis, forward
        )
        high = lax.ppermute(lax.slice_in_dim(block, 0, width, axis=dim), axis, backward)
        block = jnp.concatenate([low, block, high], axis=dim)
    return block


def cycle_geometry(row_ids, cycle_count):
    latitude = (row_ids.astype(jnp.float32) + 0.5) * (math.pi / cycle_count) - 0.5 * math.pi
    return (jnp.sin(latitude), jnp.cos(latitude))


def start_logs():
    counter = jnp.arange(LMAX).astype(jnp.float32)
    log_terms = jnp.where(
        counter > 0.0, 0.5 * jnp.log((2.0 * counter + 1.0) / jnp.maximum(2.0 * counter, 1.0)), 0.0
    )
    return jnp.cumsum(log_terms)


def next_row(degree, order_col, sine_row, prev_one, prev_two, scale_log):
    deg_gap = degree * degree - order_col * order_col
    past_one = degree >= order_col + 1.0
    past_two = degree >= order_col + 2.0
    lead_sq = jnp.where(
        past_one, (4.0 * degree * degree - 1.0) / jnp.where(past_one, deg_gap, 1.0), 0.0
    )
    lag_num = (2.0 * degree + 1.0) * ((degree - 1.0) * (degree - 1.0) - order_col * order_col)
    lag_sq = jnp.where(
        past_two, lag_num / jnp.where(past_two, (2.0 * degree - 3.0) * deg_gap, 1.0), 0.0
    )
    value_row = jnp.where(
        degree == order_col,
        1.0,
        jnp.sqrt(lead_sq) * sine_row * prev_one - jnp.sqrt(lag_sq) * prev_two,
    )
    large = jnp.abs(value_row) > rescale_limit
    factor = jnp.where(large, 1.0 / rescale_limit, 1.0)
    value_row = value_row * factor
    carried = prev_one * factor
    scale_log = scale_log + jnp.where(large, rescale_log, 0.0)
    output = value_row * jnp.exp(scale_log)
    return (value_row, carried, scale_log, output)


def wave_table(orders, part_ids, lon_ids):
    phases = (orders[:, None] * lon_ids[None, :] % NLON).astype(jnp.float32) * (
        2.0 * math.pi / NLON
    )
    return jnp.where(part_ids[:, None] == 0, jnp.cos(phases), -jnp.sin(phases))


def forward_entries(orders, part_ids, lon_ids):
    return (wave_table(orders, part_ids, lon_ids) / NLON).astype(jnp.bfloat16)


def inverse_entries(orders, part_ids, lon_ids):
    weight_gain = jnp.where(orders == 0, 1.0, 2.0)
    return (weight_gain[:, None] * wave_table(orders, part_ids, lon_ids)).astype(jnp.bfloat16)


def slot_orders(column_ids, per_owner, slot_order):
    owner_ids = column_ids // (2 * per_owner)
    part_ids = column_ids // per_owner % 2
    flat_ids = owner_ids * per_owner + column_ids % per_owner
    matches = flat_ids[:, None] == jnp.arange(LMAX, dtype=jnp.int32)[None, :]
    orders = jnp.sum(jnp.where(matches, slot_order[None, :], 0), axis=1)
    return (orders, part_ids)


def legendre_loop(orders_f, log_m, sines, cosines):
    order_col = orders_f[:, None]
    start_scale = log_m[:, None] + order_col * jnp.log(cosines)[None, :]
    sine_row = sines[None, :]
    empty = jnp.zeros(start_scale.shape, jnp.float32)
    tables = jnp.zeros((orders_f.shape[0], LMAX, sines.shape[0]), jnp.bfloat16)

    def fill_block(block_id, loop_state):
        prev_one, prev_two, scale_log, filled = loop_state
        new_rows = []
        for within in range(degree_block):
            degree = (block_id * degree_block + within).astype(jnp.float32)
            value_row, carried, scale_log, output = next_row(
                degree, order_col, sine_row, prev_one, prev_two, scale_log
            )
            prev_two = carried
            prev_one = value_row
            new_rows.append(output.astype(jnp.bfloat16))
        stacked = jnp.stack(new_rows, axis=1)
        filled = lax.dynamic_update_slice(
            filled,
            stacked,
            (jnp.int32(0), (block_id * degree_block).astype(jnp.int32), jnp.int32(0)),
        )
        return (prev_one, prev_two, scale_log, filled)

    result = lax.fori_loop(0, LMAX // degree_block, fill_block, (empty, empty, start_scale, tables))
    return result[3]


def local(
    height,
    east_vel,
    north_vel,
    sea_depth,
    sea_mask,
    forcing,
    thickness,
    cycle_length,
    slot_order,
    love_index,
    love_table,
):
    lat_rows, lon_cols = height.shape
    lat_parts = lax.axis_size("lat")
    lon_parts = lax.axis_size("lon")
    cycle_count = lat_rows * lat_parts
    per_owner = LMAX // lon_parts
    first_row = lax.axis_index("lat") * lat_rows
    first_col = lax.axis_index("lon") * lon_cols
    row_ids = first_row + jnp.arange(lat_rows, dtype=jnp.int32)
    sines, cosines = cycle_geometry(row_ids, cycle_count)
    inside = (row_ids > 0) & (row_ids < cycle_count - 1)
    wet_cells = jnp.where(inside[:, None] & (sea_mask > 0), 1.0, 0.0).astype(jnp.float32)
    level_weights = thickness / jnp.sum(thickness)
    east_push = jnp.zeros(height.shape, jnp.float32)
    north_push = jnp.zeros(height.shape, jnp.float32)
    for level in range(LEVELS):
        east_push = east_push + level_weights[level] * forcing[0, level].astype(jnp.float32)
        north_push = north_push + level_weights[level] * forcing[1, level].astype(jnp.float32)
    margin = 2 * ITERS
    stacked = jnp.stack([height, east_vel, north_vel, sea_depth, wet_cells, east_push, north_push])
    widened = padded(stacked.astype(jnp.bfloat16), (("lat", 1),), margin, False).astype(
        stacked.dtype
    )
    widened = padded(widened.astype(jnp.bfloat16), (("lon", 2),), margin, True).astype(
        widened.dtype
    )
    wide_rows = first_row - margin + jnp.arange(lat_rows + 2 * margin, dtype=jnp.int32)
    wide_sines, wide_cosines = cycle_geometry(wide_rows, cycle_count)
    coriolis = coriolis_scale * wide_sines[:, None]
    height, east, north = (widened[0], widened[1], widened[2])
    depth_wide, wet_wide, push_east, push_north = (widened[3], widened[4], widened[5], widened[6])
    for substep in range(ITERS):
        east_flux = depth_wide * east
        north_flux = depth_wide * north
        height = height[1:-1, 1:-1] - time_step * wet_wide[1:-1, 1:-1] * (
            0.5
            * (
                east_flux[1:-1, 2:]
                - east_flux[1:-1, :-2]
                + (north_flux[2:, 1:-1] - north_flux[:-2, 1:-1])
            )
        )
        east_slope = 0.5 * (height[1:-1, 2:] - height[1:-1, :-2])
        north_slope = 0.5 * (height[2:, 1:-1] - height[:-2, 1:-1])
        height = height[1:-1, 1:-1]
        east = east[2:-2, 2:-2]
        north = north[2:-2, 2:-2]
        depth_wide = depth_wide[2:-2, 2:-2]
        wet_wide = wet_wide[2:-2, 2:-2]
        push_east = push_east[2:-2, 2:-2]
        push_north = push_north[2:-2, 2:-2]
        coriolis = coriolis[2:-2]
        flow_speed = jnp.sqrt(east * east + north * north + tide_speed * tide_speed)
        damping = 1.0 + time_step * drag_coeff * flow_speed / jnp.where(
            wet_wide > 0.0, depth_wide, 1.0
        )
        east_new = (
            wet_wide * (east + time_step * (coriolis * north - east_slope + push_east)) / damping
        )
        north = (
            wet_wide * (north + time_step * (-coriolis * east - north_slope + push_north)) / damping
        )
        east = east_new
    surface_load = (wet_cells * height).astype(jnp.bfloat16)
    own_lon = first_col + jnp.arange(lon_cols, dtype=jnp.int32)
    column_ids = jnp.arange(2 * per_owner * lax.axis_size("lon"), dtype=jnp.int32)
    orders, part_ids = slot_orders(column_ids, per_owner, slot_order)
    entries = forward_entries(orders, part_ids, own_lon)
    spectra = lax.psum_scatter(
        lax.dot_general(
            entries, surface_load, (((1,), (1,)), ((), ())), preferred_element_type=jnp.float32
        ).astype(jnp.bfloat16),
        "lon",
        scatter_dimension=0,
        tiled=True,
    ).astype(jnp.float32)
    spectra = spectra.reshape(2, per_owner, lat_rows)
    own_orders = lax.dynamic_slice(slot_order, (lax.axis_index("lon") * per_owner,), (per_owner,))
    retained = own_orders[:, None] < cycle_length[None, :]
    weight_lat = 0.5 * cosines * (math.pi / cycle_count)
    weighted = jnp.where(retained[None], spectra * weight_lat[None, None, :], 0.0).astype(
        jnp.bfloat16
    )
    log_starts = start_logs()
    own_logs = jnp.sum(
        jnp.where(
            own_orders[:, None] == jnp.arange(LMAX, dtype=jnp.int32)[None, :],
            log_starts[None, :],
            0.0,
        ),
        axis=1,
    )
    tables = legendre_loop(own_orders.astype(jnp.float32), own_logs, sines, cosines)
    sums = jnp.einsum("knj,pkj->pkn", tables, weighted, preferred_element_type=jnp.float32)
    load_factor = jnp.sum(
        jnp.where(
            love_index[:, None] == jnp.arange(LOVE_ROWS, dtype=jnp.int32)[None, :],
            love_table[None, :],
            0.0,
        ),
        axis=1,
    )
    share_width = LMAX // lat_parts
    report_scale = math.sqrt(NLON * cycle_count)
    sums = lax.psum(sums, "lat")
    coefficients = sums * load_factor[None, None, :]
    scaled = coefficients.astype(jnp.bfloat16)
    own_coeffs = lax.dynamic_slice_in_dim(
        coefficients, lax.axis_index("lat") * share_width, share_width, 2
    )
    load_coeffs = report_scale * own_coeffs
    synthesis = jnp.einsum(
        "knj,pkn->pkj", tables, scaled, preferred_element_type=jnp.float32
    ).astype(jnp.bfloat16)
    synthesis = synthesis.reshape(2 * per_owner, lat_rows)
    shard_rows = lax.all_gather(synthesis, "lon", axis=0, tiled=True)
    column_ids = jnp.arange(shard_rows.shape[0], dtype=jnp.int32)
    orders, part_ids = slot_orders(column_ids, per_owner, slot_order)
    entries = inverse_entries(orders, part_ids, own_lon)
    sal_field = lax.dot_general(
        shard_rows, entries, (((0,), (0,)), ((), ())), preferred_element_type=jnp.float32
    )
    return (height, east, north, load_coeffs, sal_field)


def solution(mesh):
    in_specs = (
        P("lat", "lon"),
        P("lat", "lon"),
        P("lat", "lon"),
        P("lat", "lon"),
        P("lat", "lon"),
        P(None, None, "lat", "lon"),
        P(),
        P("lat"),
        P(),
        P(),
        P(),
    )
    out_specs = (
        P("lat", "lon"),
        P("lat", "lon"),
        P("lat", "lon"),
        P(None, "lon", "lat"),
        P("lat", "lon"),
    )
    return jax.shard_map(local, mesh=mesh, in_specs=in_specs, out_specs=out_specs, check_vma=False)
```

profile of v0, /device:TPU:0, one launch (start us, length us, event | category | flops | bytes accessed | tf_op | source)
XLA Modules:
  0.0 1059.0 jit_solution(18119053795163229721)
XLA Ops:
  16.0 10.8 %bitcast_dynamic-update-slice_fusion.1 = bf16[7,256,2160]{1,2,0:T(8,128)(2,1)S(1)} fusion(bf16[7,256,2160]{1,2,0:T(8,128)(2,1)S(1)} %get-tuple-element.550, bf16[2,8,256,2160]{2,3,1,0:T(8,128)(2,1)} %param.18, f32[]{:T(128)} %bitcast.12, f32[]{:T(128)} %bitcast.11, f32[]{:T(128)} %bitcast.10, f32[]{:T(128)} %bitcast.9, f32[]{:T(128)} %bitcast.8, ...), kind=kLoop, calls=%fused_computation.758 | loop fusion | flops 13271040 | bytes 9953312
  66.8 10.5 pad_maximum_fusion
  94.9 56.4 %concatenate.7 = bf16[7,296,2200]{1,2,0:T(8,128)(2,1)} concatenate(bf16[7,296,20]{1,2,0:T(8,128)(2,1)S(1)} %collective-permute-done.2, bf16[7,296,2160]{1,2,0:T(8,128)(2,1)} %copy-done.7, bf16[7,296,20]{1,2,0:T(8,128)(2,1)S(1)} %collective-permute-done.3), dimensions={2} | concatenate | bytes 18233600 | tf_op jit(solution)/shard_map/concatenate | solution.py:32
  151.3 13.3 %convert_element_type.790 = f32[7,296,2200]{1,2,0:T(8,128)} convert(bf16[7,296,2200]{1,2,0:T(8,128)(2,1)} %concatenate.7) | non-fusion elementwise | flops 4558400 | bytes 27350400 | tf_op jit(solution)/shard_map/convert_element_type | solution.py:164
  171.9 14.8 %slice_bitcast_fusion.1 = (f32[296,2200]{0,1:T(8,128)S(1)}, f32[296,2200]{0,1:T(8,128)}, f32[296,2200]{0,1:T(8,128)}, f32[296,2200]{0,1:T(8,128)}, f32[296,2200]...) fusion(f32[7,296,2200]{1,2,0:T(8,128)} %convert_element_type.790), kind=kLoop, calls=%fused_computation.498 | loop fusion | bytes 36467200 | tf_op jit(solution)/shard_map/squeeze | solution.py:171
  186.6 9.7 fusion.173
  196.4 13.0 %slice_multiply_fusion.11 = (f32[292,2196]{0,1:T(8,128)S(1)}, f32[292,2196]{0,1:T(8,128)}, f32[292,2196]{0,1:T(8,128)}, f32[292,2196]{0,1:T(8,128)}) fusion(f32[296,2200]{0,1:T(8,128)S(1)} %copy-done.3, f32[296,2200]{0,1:T(8,128)S(1)} %get-tuple-element.672, f32[294,2198]{0,1:T(8,128)S(1)} %fusion.173, f32[296,2200]{0,1:T(8,128)} %get-tuple-element.674, ...), kind=kLoop, calls=%fused_computation.711 | loop fusion | flops 18595728 | bytes 35911328 | tf_op jit(solution)/shard_map/mul | solution.py:173
  209.4 8.9 fusion.157
  218.2 19.6 %slice_multiply_fusion.15 = (f32[288,2192]{0,1:T(8,128)}, f32[288,2192]{0,1:T(8,128)}, f32[288,2192]{0,1:T(8,128)}, f32[288,2192]{0,1:T(8,128)}) fusion(f32[296,2200]{0,1:T(8,128)} %get-tuple-element.676, f32[296,2200]{0,1:T(8,128)S(1)} %get-tuple-element.672, f32[290,2194]{0,1:T(8,128)} %fusion.157, f32[292,2196]{0,1:T(8,128)} %get-tuple-element.684, ...), kind=kLoop, calls=%fused_computation.715 | loop fusion | flops 18307584 | bytes 35354880 | tf_op jit(solution)/shard_map/mul | solution.py:173
  237.8 11.0 %fusion.193 = f32[286,2190]{0,1:T(8,128)} fusion(f32[288,2192]{0,1:T(8,128)} %get-tuple-element.681, f32[288,2192]{0,1:T(8,128)} %get-tuple-element.542, f32[296,2200]{0,1:T(8,128)S(1)} %get-tuple-element.677, f32[290,2194]{0,1:T(8,128)} %fusion.157), kind=kLoop, calls=%fused_computation.543 | loop fusion | flops 4384380 | bytes 17537520 | tf_op jit(solution)/shard_map/sub | solution.py:175
  248.8 19.3 %slice_multiply_fusion.13 = (f32[284,2188]{0,1:T(8,128)}, f32[284,2188]{0,1:T(8,128)}, f32[284,2188]{0,1:T(8,128)}, f32[284,2188]{0,1:T(8,128)}) fusion(f32[296,2200]{0,1:T(8,128)} %get-tuple-element.676, f32[296,2200]{0,1:T(8,128)S(1)} %get-tuple-element.672, f32[286,2190]{0,1:T(8,128)} %fusion.193, f32[288,2192]{0,1:T(8,128)} %get-tuple-element.682, ...), kind=kLoop, calls=%fused_computation.713 | loop fusion | flops 18020368 | bytes 34800224 | tf_op jit(solution)/shard_map/mul | solution.py:173
  268.1 9.9 fusion.177
  278.1 12.9 %slice_multiply_fusion.19 = (f32[280,2184]{0,1:T(8,128)}, f32[280,2184]{0,1:T(8,128)}, f32[280,2184]{0,1:T(8,128)}, f32[280,2184]{0,1:T(8,128)}) fusion(f32[296,2200]{0,1:T(8,128)S(1)} %copy-done.4, f32[296,2200]{0,1:T(8,128)S(1)} %get-tuple-element.672, f32[282,2186]{0,1:T(8,128)S(1)} %fusion.177, f32[284,2188]{0,1:T(8,128)} %get-tuple-element.688, ...), kind=kLoop, calls=%fused_computation.719 | loop fusion | flops 17734080 | bytes 34247360 | tf_op jit(solution)/shard_map/mul | solution.py:173
  291.0 10.2 fusion.225
  301.2 12.7 %slice_multiply_fusion.17 = (f32[276,2180]{0,1:T(8,128)S(1)}, f32[276,2180]{0,1:T(8,128)}, f32[276,2180]{0,1:T(8,128)}, f32[276,2180]{0,1:T(8,128)}) fusion(f32[296,2200]{0,1:T(8,128)S(1)} %copy-done.4, f32[296,2200]{0,1:T(8,128)S(1)} %get-tuple-element.672, f32[278,2182]{0,1:T(8,128)S(1)} %fusion.225, f32[280,2184]{0,1:T(8,128)} %get-tuple-element.686, ...), kind=kLoop, calls=%fused_computation.717 | loop fusion | flops 17448720 | bytes 33696288 | tf_op jit(solution)/shard_map/mul | solution.py:173
  322.7 19.2 %slice_multiply_fusion.23 = (f32[272,2176]{0,1:T(8,128)}, f32[272,2176]{0,1:T(8,128)}, f32[272,2176]{0,1:T(8,128)}, f32[272,2176]{0,1:T(8,128)}) fusion(f32[296,2200]{0,1:T(8,128)} %get-tuple-element.676, f32[296,2200]{0,1:T(8,128)S(1)} %get-tuple-element.672, f32[274,2178]{0,1:T(8,128)} %fusion.209, f32[276,2180]{0,1:T(8,128)} %get-tuple-element.692, ...), kind=kLoop, calls=%fused_computation.723 | loop fusion | flops 17164288 | bytes 33147008 | tf_op jit(solution)/shard_map/mul | solution.py:173
  341.9 11.0 %fusion.257 = f32[270,2174]{0,1:T(8,128)} fusion(f32[272,2176]{0,1:T(8,128)} %get-tuple-element.689, f32[272,2176]{0,1:T(8,128)} %get-tuple-element.526, f32[296,2200]{0,1:T(8,128)S(1)} %get-tuple-element.677, f32[274,2178]{0,1:T(8,128)} %fusion.209), kind=kLoop, calls=%fused_computation.639 | loop fusion | flops 4108860 | bytes 16435440 | tf_op jit(solution)/shard_map/sub | solution.py:175
  352.9 19.3 %slice_multiply_fusion.21 = (f32[268,2172]{0,1:T(8,128)}, f32[268,2172]{0,1:T(8,128)}, f32[268,2172]{0,1:T(8,128)}, f32[268,2172]{0,1:T(8,128)}) fusion(f32[296,2200]{0,1:T(8,128)} %get-tuple-element.676, f32[296,2200]{0,1:T(8,128)S(1)} %get-tuple-element.672, f32[270,2174]{0,1:T(8,128)} %fusion.257, f32[272,2176]{0,1:T(8,128)} %get-tuple-element.690, ...), kind=kLoop, calls=%fused_computation.721 | loop fusion | flops 16880784 | bytes 32599520 | tf_op jit(solution)/shard_map/mul | solution.py:173
  372.2 11.1 %fusion.241 = f32[266,2170]{0,1:T(8,128)} fusion(f32[268,2172]{0,1:T(8,128)} %get-tuple-element.695, f32[268,2172]{0,1:T(8,128)} %get-tuple-element.522, f32[296,2200]{0,1:T(8,128)S(1)} %get-tuple-element.677, f32[270,2174]{0,1:T(8,128)} %fusion.257), kind=kLoop, calls=%fused_computation.616 | loop fusion | flops 4040540 | bytes 16162160 | tf_op jit(solution)/shard_map/sub | solution.py:175
  383.4 18.4 %slice_multiply_fusion.27 = (f32[264,2168]{0,1:T(8,128)}, f32[264,2168]{0,1:T(8,128)}, f32[264,2168]{0,1:T(8,128)}, f32[264,2168]{0,1:T(8,128)}) fusion(f32[296,2200]{0,1:T(8,128)} %get-tuple-element.676, f32[296,2200]{0,1:T(8,128)S(1)} %get-tuple-element.672, f32[266,2170]{0,1:T(8,128)} %fusion.241, f32[268,2172]{0,1:T(8,128)} %get-tuple-element.696, ...), kind=kLoop, calls=%fused_computation.727 | loop fusion | flops 16598208 | bytes 32053824 | tf_op jit(solution)/shard_map/mul | solution.py:173
  401.7 11.3 %fusion.289 = f32[262,2166]{0,1:T(8,128)} fusion(f32[264,2168]{0,1:T(8,128)} %get-tuple-element.693, f32[264,2168]{0,1:T(8,128)} %get-tuple-element.518, f32[296,2200]{0,1:T(8,128)S(1)} %get-tuple-element.677, f32[266,2170]{0,1:T(8,128)} %fusion.241), kind=kLoop, calls=%fused_computation.687 | loop fusion | flops 3972444 | bytes 15889776 | tf_op jit(solution)/shard_map/sub | solution.py:175
  413.1 19.2 %slice_multiply_fusion.25 = (f32[260,2164]{0,1:T(8,128)}, f32[260,2164]{0,1:T(8,128)}, f32[260,2164]{0,1:T(8,128)}, f32[260,2164]{0,1:T(8,128)}) fusion(f32[296,2200]{0,1:T(8,128)} %get-tuple-element.676, f32[296,2200]{0,1:T(8,128)S(1)} %get-tuple-element.672, f32[262,2166]{0,1:T(8,128)} %fusion.289, f32[264,2168]{0,1:T(8,128)} %get-tuple-element.694, ...), kind=kLoop, calls=%fused_computation.725 | loop fusion | flops 16316560 | bytes 31509920 | tf_op jit(solution)/shard_map/mul | solution.py:173
  432.3 11.0 %fusion.273 = f32[258,2162]{0,1:T(8,128)} fusion(f32[260,2164]{0,1:T(8,128)} %get-tuple-element.699, f32[260,2164]{0,1:T(8,128)} %get-tuple-element.514, f32[296,2200]{0,1:T(8,128)S(1)} %get-tuple-element.677, f32[262,2166]{0,1:T(8,128)} %fusion.289), kind=kLoop, calls=%fused_computation.664 | loop fusion | flops 3904572 | bytes 15618288 | tf_op jit(solution)/shard_map/sub | solution.py:175
  443.4 14.7 %fusion.307 = (f32[256,2160]{0,1:T(8,128)}, f32[256,2160]{0,1:T(8,128)}, f32[256,2160]{0,1:T(8,128)S(1)}) fusion(f32[296,2200]{0,1:T(8,128)S(1)} %copy-done.2, f32[258,2162]{0,1:T(8,128)} %fusion.273, f32[296,2200]{0,1:T(8,128)} %get-tuple-element.676, f32[260,2164]{0,1:T(8,128)} %get-tuple-element.700, f32[260,2164]{0,1:T(8,128)} %get-tuple-element.515, ...), kind=kLoop, calls=%fused_computation.734 | loop fusion | flops 14929920 | bytes 30967808 | tf_op jit(solution)/shard_map/div | solution.py:201
  458.9 55.8 %fusion.302 = bf16[1440,256]{1,0:T(8,128)(2,1)} fusion(s32[2160]{0:T(1024)S(1)} %copy-done.23, s32[1440]{0:T(1024)S(1)} %copy-done.20, pred[1440]{0:T(1024)(128)(4,1)S(1)} %copy-done.36, bf16[256,2160]{0,1:T(8,128)(2,1)S(1)} %fusion.394), kind=kOutput, calls=%fused_computation.728 | convolution fusion | flops 1633328640 | bytes 1859040 | tf_op jit(solution)/shard_map/dot_general | solution.py:210
  514.7 21.1 %broadcast_in_dim.923.clone = bf16[180,720,256]{2,1,0:T(8,128)(2,1)} broadcast(bf16[]{:T(256)} %constant.625.clone.1), dimensions={} | broadcast | bytes 66355200 | tf_op jit(solution)/shard_map/broadcast_in_dim | solution.py:104
  535.9 330.9 %while.23 = (s32[]{:T(128)}, f32[180,256]{1,0:T(8,128)S(1)}, f32[180,256]{1,0:T(8,128)S(1)}, f32[180,256]{1,0:T(8,128)S(1)}, bf16[180,720,256]{2,1,0:T(8,128)(2,...) while((s32[]{:T(128)}, f32[180,256]{1,0:T(8,128)S(1)}, ...), condition=%wide.region_7.8_spmd.clone, body=%wide.region_6.7_spmd.clone.sunk | while | flops 42912776 | bytes 26192132 | solution.py:125
  868.0 26.2 %convolution_bitcast_fusion = f32[2,180,720]{2,0,1:T(2,128)} fusion(bf16[180,720,256]{2,1,0:T(8,128)(2,1)} %get-tuple-element.332, f32[2,180,256]{2,1,0:T(8,128)S(1)} %reshape.2027, pred[180,256]{1,0:T(8,128)(4,1)S(1)} %broadcast_compare_fusion, f32[256]{0:T(256)S(1)} %broadcast_multiply_fusion.1), kind=kOutput, calls=%fused_computation.752 | convolution fusion | flops 132986880 | bytes 67807744 | tf_op jit(solution)/shard_map/knj,pkj->pkn/dot_general | solution.py:234
  894.4 56.9 %all-reduce.3.cloned.1.call-done = f32[2,180,720]{2,0,1:T(2,128)} async-done(((f32[2,180,720]{2,0,1:T(2,128)}), f32[2,180,720]{2,0,1:T(2,128)}) %all-reduce.3.cloned.1.call-update) | async-done | bytes 1036816 | tf_op jit(solution)/shard_map/psum | solution.py:245
  952.9 23.5 %fusion.318 = bf16[2,180,256]{2,0,1:T(2,128)(2,1)S(1)} fusion(bf16[180,720,256]{2,1,0:T(8,128)(2,1)} %get-tuple-element.332, f32[2,180,720]{2,0,1:T(2,128)S(1)} %broadcast_multiply_fusion), kind=kOutput, calls=%fused_computation.754 | convolution fusion | flops 133061760 | bytes 67576320 | tf_op jit(solution)/shard_map/knj,pkn->pkj/dot_general | solution.py:252
  977.4 18.6 %all_gather.3 = bf16[1440,256]{1,0:T(8,128)(2,1)S(1)} all-gather(bf16[360,256]{1,0:T(8,128)(2,1)S(1)} %reshape.2023), channel_id=1, replica_groups=mesh['lat'=8,'lon'=4] {'lon'}, dimensions={0}, use_global_device_ids=true | all-gather | bytes 921600 | tf_op jit(solution)/shard_map/all_gather | solution.py:256
  996.0 55.8 %fusion.150 = f32[256,2160]{0,1:T(8,128)} fusion(bf16[1440,256]{1,0:T(8,128)(2,1)S(1)} %all_gather.3, f32[1440]{0:T(1024)S(1)} %compare_select_fusion, s32[2160]{0:T(1024)S(1)} %copy-done.23, s32[1440]{0:T(1024)S(1)} %copy-done.20, pred[1440]{0:T(1024)(128)(4,1)S(1)} %copy-done.36), kind=kOutput, calls=%fused_computation.472 | convolution fusion | flops 1632960000 | bytes 2970720 | tf_op jit(solution)/shard_map/dot_general | solution.py:260
  (1498 shorter events, 409.4 us)
Async XLA Ops:
  7.2 859.8 %reduce-scatter.2.cloned.1.call-start = ((), (), s32[]{:S(2)}) async-start(), calls=%async_computation.1 | async-start | bytes 921600 | tf_op jit(solution)/shard_map/reduce_scatter | solution.py:209
  12.5 14.3 %copy-start.10 = (bf16[2,8,256,2160]{2,3,1,0:T(8,128)(2,1)S(1)}, bf16[2,8,256,2160]{2,3,1,0:T(8,128)(2,1)}, u32[]{:S(2)}) copy-start(bf16[2,8,256,2160]{2,3,1,0:T(8,128)(2,1)} %param.18) | copy-start | bytes 53084164
  43.2 12.4 %copy-start.32 = (s32[720]{0:T(1024)S(1)}, s32[720]{0:T(1024)}, u32[]{:S(2)}) copy-start(s32[720]{0:T(1024)} %param.21) | copy-start | bytes 8644
  43.2 20.2 %collective-permute-start.1 = (bf16[7,20,2160]{2,0,1:T(8,128)(2,1)S(1)}, bf16[7,20,2160]{2,0,1:T(8,128)(2,1)S(1)}, u32[]{:S(2)}, u32[]{:S(2)}) collective-permute-start(bf16[7,20,2160]{2,0,1:T(8,128)(2,1)S(1)} %copy.76), channel_id=1, source_target_pairs={{4,0},{8,4},{12,8},{16,12},{20,16},{24,20},{28,24},{5,1},{9,5},{13... | collective-permute-start | bytes 1814408 | tf_op jit(solution)/shard_map/ppermute | solution.py:31
  48.6 11.4 %collective-permute-start = (bf16[7,20,2160]{2,0,1:T(8,128)(2,1)S(1)}, bf16[7,20,2160]{2,0,1:T(8,128)(2,1)S(1)}, u32[]{:S(2)}, u32[]{:S(2)}) collective-permute-start(bf16[7,20,2160]{2,0,1:T(8,128)(2,1)S(1)} %copy.75), channel_id=1, source_target_pairs={{0,4},{4,8},{8,12},{12,16},{16,20},{20,24},{24,28},{1,5},{5,9},{9,... | collective-permute-start | bytes 1814408 | tf_op jit(solution)/shard_map/ppermute | solution.py:28
  56.2 10.6 copy-start.21
  81.7 8.9 collective-permute-start.3
  86.8 8.1 collective-permute-start.2
  186.6 9.7 copy-start.3
  268.1 9.9 copy-start.1
  268.1 9.9 copy-start.4
  341.9 11.0 %copy-start.28 = (f32[268]{0:T(512)S(1)}, f32[268]{0:T(512)}, u32[]{:S(2)}) copy-start(f32[268]{0:T(512)} %get-tuple-element.444) | copy-start | bytes 3220
  341.9 11.0 %copy-start.29 = (f32[268]{0:T(512)S(1)}, f32[268]{0:T(512)}, u32[]{:S(2)}) copy-start(f32[268]{0:T(512)} %get-tuple-element.445) | copy-start | bytes 3220
  372.2 11.1 %copy-start.26 = (f32[264]{0:T(512)S(1)}, f32[264]{0:T(512)}, u32[]{:S(2)}) copy-start(f32[264]{0:T(512)} %get-tuple-element.442) | copy-start | bytes 3172
  372.2 11.1 %copy-start.27 = (f32[264]{0:T(512)S(1)}, f32[264]{0:T(512)}, u32[]{:S(2)}) copy-start(f32[264]{0:T(512)} %get-tuple-element.443) | copy-start | bytes 3172
  401.7 11.3 %copy-start.24 = (f32[260]{0:T(512)S(1)}, f32[260]{0:T(512)}, u32[]{:S(2)}) copy-start(f32[260]{0:T(512)} %get-tuple-element.440) | copy-start | bytes 3124
  401.7 11.3 %copy-start.25 = (f32[260]{0:T(512)S(1)}, f32[260]{0:T(512)}, u32[]{:S(2)}) copy-start(f32[260]{0:T(512)} %get-tuple-element.441) | copy-start | bytes 3124
  432.3 11.0 %copy-start.2 = (f32[296,2200]{0,1:T(8,128)S(1)}, f32[296,2200]{0,1:T(8,128)}, u32[]{:S(2)}) copy-start(f32[296,2200]{0,1:T(8,128)} %get-tuple-element.673) | copy-start | bytes 7814404
  432.3 11.0 %copy-start.33 = (f32[256,1]{0,1:T(1,128)S(1)}, f32[256,1]{0,1:T(1,128)}, u32[]{:S(2)}) copy-start(f32[256,1]{0,1:T(1,128)} %get-tuple-element.706) | copy-start | bytes 3076
  432.3 11.0 %copy-start.34 = (f32[256,1]{0,1:T(1,128)S(1)}, f32[256,1]{0,1:T(1,128)}, u32[]{:S(2)}) copy-start(f32[256,1]{0,1:T(1,128)} %get-tuple-element.707) | copy-start | bytes 3076
  443.3 14.8 %copy-start.12 = (pred[256,2160]{0,1:T(8,128)(4,1)S(1)}, pred[256,2160]{0,1:T(8,128)(4,1)}, u32[]{:S(2)}) copy-start(pred[256,2160]{0,1:T(8,128)(4,1)} %get-tuple-element.551) | copy-start | bytes 1658884
  458.1 56.5 %copy-start.11 = (f32[256,2160]{0,1:T(8,128)}, f32[256,2160]{0,1:T(8,128)S(1)}, u32[]{:S(2)}) copy-start(f32[256,2160]{0,1:T(8,128)S(1)} %get-tuple-element.705) | copy-start | bytes 6635524
  514.6 436.6 %all-reduce.3.cloned.1.call-start = ((), (), s32[]{:S(2)}) async-start(), calls=%async_computation.2 | async-start | bytes 2211840 | tf_op jit(solution)/shard_map/psum | solution.py:245
  514.7 21.2 %copy-start.5 = (f32[180,256]{1,0:T(8,128)S(1)}, f32[180,256]{1,0:T(8,128)}, u32[]{:S(2)}) copy-start(f32[180,256]{1,0:T(8,128)} %custom-call.1) | copy-start | bytes 552964
  514.7 21.2 %copy-start.6 = (f32[180,256]{1,0:T(8,128)S(1)}, f32[180,256]{1,0:T(8,128)}, u32[]{:S(2)}) copy-start(f32[180,256]{1,0:T(8,128)} %custom-call) | copy-start | bytes 552964
  514.7 21.2 %copy-start.9 = (f32[180,256]{1,0:T(8,128)S(1)}, f32[180,256]{1,0:T(8,128)}, u32[]{:S(2)}) copy-start(f32[180,256]{1,0:T(8,128)} %multiply_add_fusion) | copy-start | bytes 552964
  514.7 21.2 %copy-start.17 = (f32[180]{0:T(256)S(1)}, f32[180]{0:T(256)}, u32[]{:S(2)}) copy-start(f32[180]{0:T(256)} %get-tuple-element.512) | copy-start | bytes 2164
  514.7 21.2 %copy-start.19 = (f32[180]{0:T(256)S(1)}, f32[180]{0:T(256)}, u32[]{:S(2)}) copy-start(f32[180]{0:T(256)} %copy-done.18) | copy-start | bytes 2164
  535.9 330.9 %copy-start.22 = (s32[180]{0:T(256)S(1)}, s32[180]{0:T(256)}, u32[]{:S(2)}) copy-start(s32[180]{0:T(256)} %copy-done.21) | copy-start | bytes 2164
  535.9 330.9 %copy-start.37 = (s32[256]{0:T(256)S(1)}, s32[256]{0:T(256)}, u32[]{:S(2)}) copy-start(s32[256]{0:T(256)} %param.20) | copy-start | bytes 3076
  867.9 26.3 %copy-start.35 = (s32[720]{0:T(1024)S(1)}, s32[720]{0:T(1024)}, u32[]{:S(2)}) copy-start(s32[720]{0:T(1024)} %param.22) | copy-start | bytes 8644
  867.9 26.3 %copy-start.38 = (f32[64]{0:T(128)S(1)}, f32[64]{0:T(128)}, u32[]{:S(2)}) copy-start(f32[64]{0:T(128)} %param.23) | copy-start | bytes 772
  (13 other events, 52.0 us)
Sparse Core Ops, SparseCore 0:
  514.8 22.8 reduce-scatter.1
  894.3 56.8 all-reduce.2
where the time goes:
time: 1070 us; the launch traced here: 1060 us
  other arithmetic  604 us (56%)
  local copies, waits for them, and re-layouts  178 us (17%)
  matrix products  161 us (15%)
  waiting for transfers between devices  64.3 us (6%)
  blocking collectives  18.6 us (2%)
  between operations  15.1 us (1%)
    while x690, other arithmetic  226 us
    mul x10, other arithmetic, local(): east_flux = depth_wide * east  161 us
    sub x10, other arithmetic, local(): height[1:-1, 1:-1]  103 us
    psum x1, waiting for transfers between devices, local(): sums = lax.psum(sums, 'lat')  56.9 us
    dynamic_update_slice x30, local copies, waits for them, and re-layouts, fill_block(): lax.dynamic_update_slice(filled, stacked, (jnp.int32(0), (block_id * degr...  56.7 us
    concatenate x1, local copies, waits for them, and re-layouts, padded(): block = jnp.concatenate([low, block, high], axis=dim)  56.4 us
    dot_general x1, matrix products, local(): lax.dot_general(shard_rows, entries, (((0,), (0,)), ((), ())), preferred_...  55.8 us
    dot_general x1, matrix products, local(): lax.dot_general(entries, surface_load, (((1,), (1,)), ((), ())), preferre...  55.8 us
  transfers between devices with their start and end apart: 6, of which 3 were waited for; matrix products, arithmetic and copies ran while one was open for 34% of the time, Pallas kernels for 0%

commit v1 on v0

--- a/solution.py
+++ b/solution.py
@@ -242,7 +242,12 @@
     )
     share_width = LMAX // lat_parts
     report_scale = math.sqrt(NLON * cycle_count)
-    sums = lax.psum(sums, "lat")
+    peers = lax.axis_size("lat")
+    acc, far = (sums, 1)
+    while far < peers:
+        acc = acc + lax.ppermute(acc, "lat", [(i_2, i_2 ^ far) for i_2 in range(peers)])
+        far = 2 * far
+    sums = acc
     coefficients = sums * load_factor[None, None, :]
     scaled = coefficients.astype(jnp.bfloat16)
     own_coeffs = lax.dynamic_slice_in_dim(

time: 1070 us -> 1070 us (level)
    psum x1 -> x0, waiting for transfers between devices: 56.9 us -> none  [local(): sums = lax.psum(sums, 'lat')]
    ppermute x0 -> x3, waiting for transfers between devices: none -> 51.2 us  [local(): lax.ppermute(acc, 'lat', [(i_2, i_2 ^ far) for i_2 in range(peers)])]
  transfers between devices with their start and end apart: 6 -> 8, of which waited for: 3 -> 5; matrix products, arithmetic and copies ran while one was open for 34% -> 34% of each run, Pallas kernels for 0% -> 0%
where the time goes in v1:
time: 1070 us; the launch traced here: 1060 us
  other arithmetic  604 us (56%)
  local copies, waits for them, and re-layouts  178 us (17%)
  matrix products  160 us (15%)
  waiting for transfers between devices  58.5 us (5%)
  blocking collectives  17.1 us (2%)
  starting transfers between devices  15.3 us (1%)
  between operations  15.1 us (1%)
    while x690, other arithmetic  226 us
    mul x10, other arithmetic, local(): east_flux = depth_wide * east  161 us
    sub x10, other arithmetic, local(): height[1:-1, 1:-1]  103 us
    dynamic_update_slice x30, local copies, waits for them, and re-layouts, fill_block(): lax.dynamic_update_slice(filled, stacked, (jnp.int32(0), (block_id * degr...  56.7 us
    concatenate x1, local copies, waits for them, and re-layouts, padded(): block = jnp.concatenate([low, block, high], axis=dim)  56.4 us
    dot_general x1, matrix products, local(): lax.dot_general(shard_rows, entries, (((0,), (0,)), ((), ())), preferred_...  55.8 us
    dot_general x1, matrix products, local(): lax.dot_general(entries, surface_load, (((1,), (1,)), ((), ())), preferre...  55.7 us
    ppermute x3, waiting for transfers between devices, local(): lax.ppermute(acc, 'lat', [(i_2, i_2 ^ far) for i_2 in range(peers)])  51.2 us
  transfers between devices with their start and end apart: 8, of which 5 were waited for; matrix products, arithmetic and copies ran while one was open for 34% of the time, Pallas kernels for 0%

profile of v1, /device:TPU:0, one launch (start us, length us, event | category | flops | bytes accessed | tf_op | source)
XLA Modules:
  0.0 1056.4 jit_solution(10525184374630752660)
XLA Ops:
  16.0 10.8 %bitcast_dynamic-update-slice_fusion.1 = bf16[7,256,2160]{1,2,0:T(8,128)(2,1)S(1)} fusion(bf16[7,256,2160]{1,2,0:T(8,128)(2,1)S(1)} %get-tuple-element.550, bf16[2,8,256,2160]{2,3,1,0:T(8,128)(2,1)} %param.18, f32[]{:T(128)} %bitcast.12, f32[]{:T(128)} %bitcast.11, f32[]{:T(128)} %bitcast.10, f32[]{:T(128)} %bitcast.9, f32[]{:T(128)} %bitcast.8, ...), kind=kLoop, calls=%fused_computation.758 | loop fusion | flops 13271040 | bytes 9953312
  66.8 10.5 pad_maximum_fusion
  94.9 56.4 %concatenate.7 = bf16[7,296,2200]{1,2,0:T(8,128)(2,1)} concatenate(bf16[7,296,20]{1,2,0:T(8,128)(2,1)S(1)} %collective-permute-done.2, bf16[7,296,2160]{1,2,0:T(8,128)(2,1)} %copy-done.7, bf16[7,296,20]{1,2,0:T(8,128)(2,1)S(1)} %collective-permute-done.3), dimensions={2} | concatenate | bytes 18233600 | tf_op jit(solution)/shard_map/concatenate | solution.py:32
  151.3 13.3 %convert_element_type.790 = f32[7,296,2200]{1,2,0:T(8,128)} convert(bf16[7,296,2200]{1,2,0:T(8,128)(2,1)} %concatenate.7) | non-fusion elementwise | flops 4558400 | bytes 27350400 | tf_op jit(solution)/shard_map/convert_element_type | solution.py:164
  171.9 14.8 %slice_bitcast_fusion.1 = (f32[296,2200]{0,1:T(8,128)S(1)}, f32[296,2200]{0,1:T(8,128)}, f32[296,2200]{0,1:T(8,128)}, f32[296,2200]{0,1:T(8,128)}, f32[296,2200]...) fusion(f32[7,296,2200]{1,2,0:T(8,128)} %convert_element_type.790), kind=kLoop, calls=%fused_computation.498 | loop fusion | bytes 36467200 | tf_op jit(solution)/shard_map/squeeze | solution.py:171
  186.7 9.7 fusion.173
  196.4 13.0 %slice_multiply_fusion.11 = (f32[292,2196]{0,1:T(8,128)S(1)}, f32[292,2196]{0,1:T(8,128)}, f32[292,2196]{0,1:T(8,128)}, f32[292,2196]{0,1:T(8,128)}) fusion(f32[296,2200]{0,1:T(8,128)S(1)} %copy-done.3, f32[296,2200]{0,1:T(8,128)S(1)} %get-tuple-element.672, f32[294,2198]{0,1:T(8,128)S(1)} %fusion.173, f32[296,2200]{0,1:T(8,128)} %get-tuple-element.674, ...), kind=kLoop, calls=%fused_computation.711 | loop fusion | flops 18595728 | bytes 35911328 | tf_op jit(solution)/shard_map/mul | solution.py:173
  218.3 19.8 %slice_multiply_fusion.15 = (f32[288,2192]{0,1:T(8,128)}, f32[288,2192]{0,1:T(8,128)}, f32[288,2192]{0,1:T(8,128)}, f32[288,2192]{0,1:T(8,128)}) fusion(f32[296,2200]{0,1:T(8,128)} %get-tuple-element.676, f32[296,2200]{0,1:T(8,128)S(1)} %get-tuple-element.672, f32[290,2194]{0,1:T(8,128)} %fusion.157, f32[292,2196]{0,1:T(8,128)} %get-tuple-element.684, ...), kind=kLoop, calls=%fused_computation.715 | loop fusion | flops 18307584 | bytes 35354880 | tf_op jit(solution)/shard_map/mul | solution.py:173
  238.0 11.0 %fusion.193 = f32[286,2190]{0,1:T(8,128)} fusion(f32[288,2192]{0,1:T(8,128)} %get-tuple-element.681, f32[288,2192]{0,1:T(8,128)} %get-tuple-element.542, f32[296,2200]{0,1:T(8,128)S(1)} %get-tuple-element.677, f32[290,2194]{0,1:T(8,128)} %fusion.157), kind=kLoop, calls=%fused_computation.543 | loop fusion | flops 4384380 | bytes 17537520 | tf_op jit(solution)/shard_map/sub | solution.py:175
  249.0 19.2 %slice_multiply_fusion.13 = (f32[284,2188]{0,1:T(8,128)}, f32[284,2188]{0,1:T(8,128)}, f32[284,2188]{0,1:T(8,128)}, f32[284,2188]{0,1:T(8,128)}) fusion(f32[296,2200]{0,1:T(8,128)} %get-tuple-element.676, f32[296,2200]{0,1:T(8,128)S(1)} %get-tuple-element.672, f32[286,2190]{0,1:T(8,128)} %fusion.193, f32[288,2192]{0,1:T(8,128)} %get-tuple-element.682, ...), kind=kLoop, calls=%fused_computation.713 | loop fusion | flops 18020368 | bytes 34800224 | tf_op jit(solution)/shard_map/mul | solution.py:173
  268.3 9.9 fusion.177
  278.2 12.9 %slice_multiply_fusion.19 = (f32[280,2184]{0,1:T(8,128)}, f32[280,2184]{0,1:T(8,128)}, f32[280,2184]{0,1:T(8,128)}, f32[280,2184]{0,1:T(8,128)}) fusion(f32[296,2200]{0,1:T(8,128)S(1)} %copy-done.4, f32[296,2200]{0,1:T(8,128)S(1)} %get-tuple-element.672, f32[282,2186]{0,1:T(8,128)S(1)} %fusion.177, f32[284,2188]{0,1:T(8,128)} %get-tuple-element.688, ...), kind=kLoop, calls=%fused_computation.719 | loop fusion | flops 17734080 | bytes 34247360 | tf_op jit(solution)/shard_map/mul | solution.py:173
  291.1 9.9 fusion.225
  301.1 12.7 %slice_multiply_fusion.17 = (f32[276,2180]{0,1:T(8,128)S(1)}, f32[276,2180]{0,1:T(8,128)}, f32[276,2180]{0,1:T(8,128)}, f32[276,2180]{0,1:T(8,128)}) fusion(f32[296,2200]{0,1:T(8,128)S(1)} %copy-done.4, f32[296,2200]{0,1:T(8,128)S(1)} %get-tuple-element.672, f32[278,2182]{0,1:T(8,128)S(1)} %fusion.225, f32[280,2184]{0,1:T(8,128)} %get-tuple-element.686, ...), kind=kLoop, calls=%fused_computation.717 | loop fusion | flops 17448720 | bytes 33696288 | tf_op jit(solution)/shard_map/mul | solution.py:173
  322.6 19.4 %slice_multiply_fusion.23 = (f32[272,2176]{0,1:T(8,128)}, f32[272,2176]{0,1:T(8,128)}, f32[272,2176]{0,1:T(8,128)}, f32[272,2176]{0,1:T(8,128)}) fusion(f32[296,2200]{0,1:T(8,128)} %get-tuple-element.676, f32[296,2200]{0,1:T(8,128)S(1)} %get-tuple-element.672, f32[274,2178]{0,1:T(8,128)} %fusion.209, f32[276,2180]{0,1:T(8,128)} %get-tuple-element.692, ...), kind=kLoop, calls=%fused_computation.723 | loop fusion | flops 17164288 | bytes 33147008 | tf_op jit(solution)/shard_map/mul | solution.py:173
  342.0 11.0 %fusion.257 = f32[270,2174]{0,1:T(8,128)} fusion(f32[272,2176]{0,1:T(8,128)} %get-tuple-element.689, f32[272,2176]{0,1:T(8,128)} %get-tuple-element.526, f32[296,2200]{0,1:T(8,128)S(1)} %get-tuple-element.677, f32[274,2178]{0,1:T(8,128)} %fusion.209), kind=kLoop, calls=%fused_computation.639 | loop fusion | flops 4108860 | bytes 16435440 | tf_op jit(solution)/shard_map/sub | solution.py:175
  353.1 19.2 %slice_multiply_fusion.21 = (f32[268,2172]{0,1:T(8,128)}, f32[268,2172]{0,1:T(8,128)}, f32[268,2172]{0,1:T(8,128)}, f32[268,2172]{0,1:T(8,128)}) fusion(f32[296,2200]{0,1:T(8,128)} %get-tuple-element.676, f32[296,2200]{0,1:T(8,128)S(1)} %get-tuple-element.672, f32[270,2174]{0,1:T(8,128)} %fusion.257, f32[272,2176]{0,1:T(8,128)} %get-tuple-element.690, ...), kind=kLoop, calls=%fused_computation.721 | loop fusion | flops 16880784 | bytes 32599520 | tf_op jit(solution)/shard_map/mul | solution.py:173
  372.3 11.1 %fusion.241 = f32[266,2170]{0,1:T(8,128)} fusion(f32[268,2172]{0,1:T(8,128)} %get-tuple-element.695, f32[268,2172]{0,1:T(8,128)} %get-tuple-element.522, f32[296,2200]{0,1:T(8,128)S(1)} %get-tuple-element.677, f32[270,2174]{0,1:T(8,128)} %fusion.257), kind=kLoop, calls=%fused_computation.616 | loop fusion | flops 4040540 | bytes 16162160 | tf_op jit(solution)/shard_map/sub | solution.py:175
  383.4 18.4 %slice_multiply_fusion.27 = (f32[264,2168]{0,1:T(8,128)}, f32[264,2168]{0,1:T(8,128)}, f32[264,2168]{0,1:T(8,128)}, f32[264,2168]{0,1:T(8,128)}) fusion(f32[296,2200]{0,1:T(8,128)} %get-tuple-element.676, f32[296,2200]{0,1:T(8,128)S(1)} %get-tuple-element.672, f32[266,2170]{0,1:T(8,128)} %fusion.241, f32[268,2172]{0,1:T(8,128)} %get-tuple-element.696, ...), kind=kLoop, calls=%fused_computation.727 | loop fusion | flops 16598208 | bytes 32053824 | tf_op jit(solution)/shard_map/mul | solution.py:173
  401.8 11.1 %fusion.289 = f32[262,2166]{0,1:T(8,128)} fusion(f32[264,2168]{0,1:T(8,128)} %get-tuple-element.693, f32[264,2168]{0,1:T(8,128)} %get-tuple-element.518, f32[296,2200]{0,1:T(8,128)S(1)} %get-tuple-element.677, f32[266,2170]{0,1:T(8,128)} %fusion.241), kind=kLoop, calls=%fused_computation.687 | loop fusion | flops 3972444 | bytes 15889776 | tf_op jit(solution)/shard_map/sub | solution.py:175
  413.0 19.2 %slice_multiply_fusion.25 = (f32[260,2164]{0,1:T(8,128)}, f32[260,2164]{0,1:T(8,128)}, f32[260,2164]{0,1:T(8,128)}, f32[260,2164]{0,1:T(8,128)}) fusion(f32[296,2200]{0,1:T(8,128)} %get-tuple-element.676, f32[296,2200]{0,1:T(8,128)S(1)} %get-tuple-element.672, f32[262,2166]{0,1:T(8,128)} %fusion.289, f32[264,2168]{0,1:T(8,128)} %get-tuple-element.694, ...), kind=kLoop, calls=%fused_computation.725 | loop fusion | flops 16316560 | bytes 31509920 | tf_op jit(solution)/shard_map/mul | solution.py:173
  432.2 11.0 %fusion.273 = f32[258,2162]{0,1:T(8,128)} fusion(f32[260,2164]{0,1:T(8,128)} %get-tuple-element.699, f32[260,2164]{0,1:T(8,128)} %get-tuple-element.514, f32[296,2200]{0,1:T(8,128)S(1)} %get-tuple-element.677, f32[262,2166]{0,1:T(8,128)} %fusion.289), kind=kLoop, calls=%fused_computation.664 | loop fusion | flops 3904572 | bytes 15618288 | tf_op jit(solution)/shard_map/sub | solution.py:175
  443.3 15.0 %fusion.307 = (f32[256,2160]{0,1:T(8,128)}, f32[256,2160]{0,1:T(8,128)}, f32[256,2160]{0,1:T(8,128)S(1)}) fusion(f32[296,2200]{0,1:T(8,128)S(1)} %copy-done.2, f32[258,2162]{0,1:T(8,128)} %fusion.273, f32[296,2200]{0,1:T(8,128)} %get-tuple-element.676, f32[260,2164]{0,1:T(8,128)} %get-tuple-element.700, f32[260,2164]{0,1:T(8,128)} %get-tuple-element.515, ...), kind=kLoop, calls=%fused_computation.734 | loop fusion | flops 14929920 | bytes 30967808 | tf_op jit(solution)/shard_map/div | solution.py:201
  459.0 55.7 %fusion.302 = bf16[1440,256]{1,0:T(8,128)(2,1)} fusion(s32[2160]{0:T(1024)S(1)} %copy-done.23, s32[1440]{0:T(1024)S(1)} %copy-done.20, pred[1440]{0:T(1024)(128)(4,1)S(1)} %copy-done.36, bf16[256,2160]{0,1:T(8,128)(2,1)S(1)} %fusion.394), kind=kOutput, calls=%fused_computation.728 | convolution fusion | flops 1633328640 | bytes 1859040 | tf_op jit(solution)/shard_map/dot_general | solution.py:210
  514.8 20.9 %broadcast_in_dim.923.clone = bf16[180,720,256]{2,1,0:T(8,128)(2,1)} broadcast(bf16[]{:T(256)} %constant.625.clone.1), dimensions={} | broadcast | bytes 66355200 | tf_op jit(solution)/shard_map/broadcast_in_dim | solution.py:104
  535.8 331.0 %while.23 = (s32[]{:T(128)}, f32[180,256]{1,0:T(8,128)S(1)}, f32[180,256]{1,0:T(8,128)S(1)}, f32[180,256]{1,0:T(8,128)S(1)}, bf16[180,720,256]{2,1,0:T(8,128)(2,...) while((s32[]{:T(128)}, f32[180,256]{1,0:T(8,128)S(1)}, ...), condition=%wide.region_7.8_spmd.clone, body=%wide.region_6.7_spmd.clone.sunk | while | flops 42912776 | bytes 26192132 | solution.py:125
  868.0 25.3 %convolution_bitcast_fusion = f32[2,180,720]{2,0,1:T(2,128)S(1)} fusion(bf16[180,720,256]{2,1,0:T(8,128)(2,1)} %get-tuple-element.332, f32[2,180,256]{2,1,0:T(8,128)S(1)} %reshape.2027, pred[180,256]{1,0:T(8,128)(4,1)S(1)} %broadcast_compare_fusion, f32[256]{0:T(256)S(1)} %broadcast_multiply_fusion), kind=kOutput, calls=%fused_computation.752 | convolution fusion | flops 132986880 | bytes 67807744 | tf_op jit(solution)/shard_map/knj,pkj->pkn/dot_general | solution.py:234
  899.1 24.7 %collective-permute-done.5 = f32[2,180,720]{2,0,1:T(2,128)S(1)} collective-permute-done((f32[2,180,720]{2,0,1:T(2,128)S(1)}, f32[2,180,720]{2,0,1:T(2,128)S(1)}, u32[]{:S(2)}, u32[]{:S(2)}) %collective-permute-start.5) | collective-permute-done | bytes 1036832 | tf_op jit(solution)/shard_map/ppermute | solution.py:248
  927.6 23.7 %collective-permute-done.6 = f32[2,180,720]{2,0,1:T(2,128)S(1)} collective-permute-done((f32[2,180,720]{2,0,1:T(2,128)S(1)}, f32[2,180,720]{2,0,1:T(2,128)S(1)}, u32[]{:S(2)}, u32[]{:S(2)}) %collective-permute-start.6) | collective-permute-done | bytes 1036832 | tf_op jit(solution)/shard_map/ppermute | solution.py:248
  951.9 23.5 %fusion.318 = bf16[2,180,256]{2,0,1:T(2,128)(2,1)S(1)} fusion(bf16[180,720,256]{2,1,0:T(8,128)(2,1)} %get-tuple-element.332, f32[2,180,720]{2,0,1:T(2,128)S(1)} %add_multiply_fusion), kind=kOutput, calls=%fused_computation.754 | convolution fusion | flops 133061760 | bytes 67576320 | tf_op jit(solution)/shard_map/knj,pkn->pkj/dot_general | solution.py:257
  976.4 17.1 %all_gather.3 = bf16[1440,256]{1,0:T(8,128)(2,1)S(1)} all-gather(bf16[360,256]{1,0:T(8,128)(2,1)S(1)} %reshape.2023), channel_id=1, replica_groups=mesh['lat'=8,'lon'=4] {'lon'}, dimensions={0}, use_global_device_ids=true | all-gather | bytes 921600 | tf_op jit(solution)/shard_map/all_gather | solution.py:261
  993.4 55.8 %fusion.150 = f32[256,2160]{0,1:T(8,128)} fusion(bf16[1440,256]{1,0:T(8,128)(2,1)S(1)} %all_gather.3, f32[1440]{0:T(1024)S(1)} %compare_select_fusion, s32[2160]{0:T(1024)S(1)} %copy-done.23, s32[1440]{0:T(1024)S(1)} %copy-done.20, pred[1440]{0:T(1024)(128)(4,1)S(1)} %copy-done.36), kind=kOutput, calls=%fused_computation.472 | convolution fusion | flops 1632960000 | bytes 2970720 | tf_op jit(solution)/shard_map/dot_general | solution.py:265
  (1503 shorter events, 426.7 us)
Async XLA Ops:
  7.2 859.8 %reduce-scatter.2.cloned.1.call-start = ((), (), s32[]{:S(2)}) async-start(), calls=%async_computation.1 | async-start | bytes 921600 | tf_op jit(solution)/shard_map/reduce_scatter | solution.py:209
  12.5 14.3 %copy-start.10 = (bf16[2,8,256,2160]{2,3,1,0:T(8,128)(2,1)S(1)}, bf16[2,8,256,2160]{2,3,1,0:T(8,128)(2,1)}, u32[]{:S(2)}) copy-start(bf16[2,8,256,2160]{2,3,1,0:T(8,128)(2,1)} %param.18) | copy-start | bytes 53084164
  43.2 12.4 %copy-start.32 = (s32[720]{0:T(1024)S(1)}, s32[720]{0:T(1024)}, u32[]{:S(2)}) copy-start(s32[720]{0:T(1024)} %param.21) | copy-start | bytes 8644
  43.2 20.2 %collective-permute-start.1 = (bf16[7,20,2160]{2,0,1:T(8,128)(2,1)S(1)}, bf16[7,20,2160]{2,0,1:T(8,128)(2,1)S(1)}, u32[]{:S(2)}, u32[]{:S(2)}) collective-permute-start(bf16[7,20,2160]{2,0,1:T(8,128)(2,1)S(1)} %copy.76), channel_id=1, source_target_pairs={{4,0},{8,4},{12,8},{16,12},{20,16},{24,20},{28,24},{5,1},{9,5},{13... | collective-permute-start | bytes 1814408 | tf_op jit(solution)/shard_map/ppermute | solution.py:31
  48.6 11.4 %collective-permute-start = (bf16[7,20,2160]{2,0,1:T(8,128)(2,1)S(1)}, bf16[7,20,2160]{2,0,1:T(8,128)(2,1)S(1)}, u32[]{:S(2)}, u32[]{:S(2)}) collective-permute-start(bf16[7,20,2160]{2,0,1:T(8,128)(2,1)S(1)} %copy.75), channel_id=1, source_target_pairs={{0,4},{4,8},{8,12},{12,16},{16,20},{20,24},{24,28},{1,5},{5,9},{9,... | collective-permute-start | bytes 1814408 | tf_op jit(solution)/shard_map/ppermute | solution.py:28
  56.2 10.6 copy-start.21
  81.7 8.9 collective-permute-start.3
  86.8 8.1 collective-permute-start.2
  268.3 9.9 copy-start.4
  342.0 11.0 %copy-start.28 = (f32[268]{0:T(512)S(1)}, f32[268]{0:T(512)}, u32[]{:S(2)}) copy-start(f32[268]{0:T(512)} %get-tuple-element.444) | copy-start | bytes 3220
  342.0 11.0 %copy-start.29 = (f32[268]{0:T(512)S(1)}, f32[268]{0:T(512)}, u32[]{:S(2)}) copy-start(f32[268]{0:T(512)} %get-tuple-element.445) | copy-start | bytes 3220
  372.3 11.1 %copy-start.26 = (f32[264]{0:T(512)S(1)}, f32[264]{0:T(512)}, u32[]{:S(2)}) copy-start(f32[264]{0:T(512)} %get-tuple-element.442) | copy-start | bytes 3172
  372.3 11.1 %copy-start.27 = (f32[264]{0:T(512)S(1)}, f32[264]{0:T(512)}, u32[]{:S(2)}) copy-start(f32[264]{0:T(512)} %get-tuple-element.443) | copy-start | bytes 3172
  401.8 11.2 %copy-start.24 = (f32[260]{0:T(512)S(1)}, f32[260]{0:T(512)}, u32[]{:S(2)}) copy-start(f32[260]{0:T(512)} %get-tuple-element.440) | copy-start | bytes 3124
  401.8 11.2 %copy-start.25 = (f32[260]{0:T(512)S(1)}, f32[260]{0:T(512)}, u32[]{:S(2)}) copy-start(f32[260]{0:T(512)} %get-tuple-element.441) | copy-start | bytes 3124
  432.2 11.0 %copy-start.2 = (f32[296,2200]{0,1:T(8,128)S(1)}, f32[296,2200]{0,1:T(8,128)}, u32[]{:S(2)}) copy-start(f32[296,2200]{0,1:T(8,128)} %get-tuple-element.673) | copy-start | bytes 7814404
  432.2 11.0 %copy-start.33 = (f32[256,1]{0,1:T(1,128)S(1)}, f32[256,1]{0,1:T(1,128)}, u32[]{:S(2)}) copy-start(f32[256,1]{0,1:T(1,128)} %get-tuple-element.706) | copy-start | bytes 3076
  432.2 11.0 %copy-start.34 = (f32[256,1]{0,1:T(1,128)S(1)}, f32[256,1]{0,1:T(1,128)}, u32[]{:S(2)}) copy-start(f32[256,1]{0,1:T(1,128)} %get-tuple-element.707) | copy-start | bytes 3076
  443.2 15.0 %copy-start.12 = (pred[256,2160]{0,1:T(8,128)(4,1)S(1)}, pred[256,2160]{0,1:T(8,128)(4,1)}, u32[]{:S(2)}) copy-start(pred[256,2160]{0,1:T(8,128)(4,1)} %get-tuple-element.551) | copy-start | bytes 1658884
  458.2 56.5 %copy-start.11 = (f32[256,2160]{0,1:T(8,128)}, f32[256,2160]{0,1:T(8,128)S(1)}, u32[]{:S(2)}) copy-start(f32[256,2160]{0,1:T(8,128)S(1)} %get-tuple-element.705) | copy-start | bytes 6635524
  514.8 21.0 %copy-start.5 = (f32[180,256]{1,0:T(8,128)S(1)}, f32[180,256]{1,0:T(8,128)}, u32[]{:S(2)}) copy-start(f32[180,256]{1,0:T(8,128)} %custom-call.1) | copy-start | bytes 552964
  514.8 20.9 %copy-start.6 = (f32[180,256]{1,0:T(8,128)S(1)}, f32[180,256]{1,0:T(8,128)}, u32[]{:S(2)}) copy-start(f32[180,256]{1,0:T(8,128)} %custom-call) | copy-start | bytes 552964
  514.8 20.9 %copy-start.9 = (f32[180,256]{1,0:T(8,128)S(1)}, f32[180,256]{1,0:T(8,128)}, u32[]{:S(2)}) copy-start(f32[180,256]{1,0:T(8,128)} %multiply_add_fusion) | copy-start | bytes 552964
  514.8 20.9 %copy-start.17 = (f32[180]{0:T(256)S(1)}, f32[180]{0:T(256)}, u32[]{:S(2)}) copy-start(f32[180]{0:T(256)} %get-tuple-element.512) | copy-start | bytes 2164
  514.8 20.9 %copy-start.19 = (f32[180]{0:T(256)S(1)}, f32[180]{0:T(256)}, u32[]{:S(2)}) copy-start(f32[180]{0:T(256)} %copy-done.18) | copy-start | bytes 2164
  535.7 331.1 %copy-start.22 = (s32[180]{0:T(256)S(1)}, s32[180]{0:T(256)}, u32[]{:S(2)}) copy-start(s32[180]{0:T(256)} %copy-done.21) | copy-start | bytes 2164
  535.8 331.1 %copy-start.37 = (s32[256]{0:T(256)S(1)}, s32[256]{0:T(256)}, u32[]{:S(2)}) copy-start(s32[256]{0:T(256)} %param.20) | copy-start | bytes 3076
  893.2 34.2 %copy-start.35 = (s32[720]{0:T(1024)S(1)}, s32[720]{0:T(1024)}, u32[]{:S(2)}) copy-start(s32[720]{0:T(1024)} %param.22) | copy-start | bytes 8644
  893.2 34.2 %copy-start.38 = (f32[64]{0:T(128)S(1)}, f32[64]{0:T(128)}, u32[]{:S(2)}) copy-start(f32[64]{0:T(128)} %param.23) | copy-start | bytes 772
  893.2 2.8 collective-permute-start.4
  896.6 27.1 %collective-permute-start.5 = (f32[2,180,720]{2,0,1:T(2,128)S(1)}, f32[2,180,720]{2,0,1:T(2,128)S(1)}, u32[]{:S(2)}, u32[]{:S(2)}) collective-permute-start(f32[2,180,720]{2,0,1:T(2,128)S(1)} %add.2504), channel_id=1, source_target_pairs={{0,8},{4,12},{8,0},{12,4},{16,24},{20,28},{24,16},{28,20},{1,9},{5... | collective-permute-start | bytes 3110408 | tf_op jit(solution)/shard_map/ppermute | solution.py:248
  924.3 27.0 %collective-permute-start.6 = (f32[2,180,720]{2,0,1:T(2,128)S(1)}, f32[2,180,720]{2,0,1:T(2,128)S(1)}, u32[]{:S(2)}, u32[]{:S(2)}) collective-permute-start(f32[2,180,720]{2,0,1:T(2,128)S(1)} %add.2505), channel_id=1, source_target_pairs={{0,16},{4,20},{8,24},{12,28},{16,0},{20,4},{24,8},{28,12},{1,17},{... | collective-permute-start | bytes 3110408 | tf_op jit(solution)/shard_map/ppermute | solution.py:248
  (15 other events, 71.6 us)
Sparse Core Ops, SparseCore 0:
  514.9 22.8 reduce-scatter.1
